TPU v7x, 32 devices: a whole 2x2x4 slice. The times are simulated.
32 devices in a mesh: ph: 4 (over x, core), ka: 8 (over z, y).
Axes of the slice: x: 2, y: 2, z: 4, core: 2. Of those that a mesh axis runs over, the one named last changes fastest.
Arguments:
- g_wan: bfloat16 [32, 48, 48, 2, 1024], P('ka', 'ph'), may hold values from -6 to 6
- el_cells: int32 [3, 32], replicated, may hold values from -6 to 6
- ph_cells: int32 [3, 48], P(None, 'ph'), may hold values from -4 to 4
- q_point: int32 [3], replicated, may hold values from 0 to 63
- kpoints: int32 [3, 2048], P(None, 'ka'), may hold values from 0 to 63
- eigvec: float32 [2, 48, 48], replicated, may hold values from -0.875 to 0.875
- omega: float32 [48], replicated, may hold values from 0.25 to 4
Outputs:
- strength: float32 [48, 32, 2048], P('ph', None, 'ka')
All inputs are finite; a program needn't handle non-finite values.
Results may differ from a plain program's by a relative error of at most 0.0018.
Values may be sent and summed in bfloat16 or wider, within the bound.
A program may use at most 128 MiB of HBM per device.

v0:
```python
import math

import jax
import jax.numpy as jnp
from jax import lax
from jax.sharding import PartitionSpec as P

W = 32
KGRID = 64


def angles(numerators, vectors):
    summed = jnp.sum(numerators[:, :, None] * vectors[:, None, :], axis=0)
    return jnp.mod(summed, KGRID).astype(jnp.float32) * (2.0 * math.pi / KGRID)


def coupling(q_angle, eigvec, omega):
    mode_scale = 1.0 / jnp.sqrt(2.0 * omega)
    cos_phase = jnp.cos(q_angle)[:, None, None]
    sin_phase = jnp.sin(q_angle)[:, None, None]
    real_part = eigvec[0][None]
    imag_part = eigvec[1][None]
    coef_re = ((cos_phase * real_part - sin_phase * imag_part) * mode_scale).astype(jnp.bfloat16)
    coef_im = ((sin_phase * real_part + cos_phase * imag_part) * mode_scale).astype(jnp.bfloat16)
    return jnp.stack([jnp.stack([coef_re, coef_im], 2), jnp.stack([-coef_im, coef_re], 2)], 2)


def stacked(mode_block):
    row_count = mode_block.shape[0]
    vert_re = mode_block[:, :, 0, :].reshape(row_count, -1)
    vert_im = mode_block[:, :, 1, :].reshape(row_count, -1)
    upper = jnp.concatenate([vert_re, vert_im], 1)
    lower = jnp.concatenate([-vert_im, vert_re], 1)
    return jnp.concatenate([upper, lower], 0)


def pair_strength(bloch_sum, mode_count, normalizer):
    k_count = bloch_sum.shape[0]
    half_width = bloch_sum.shape[1] // 2
    bloch_re = bloch_sum[:, :half_width].reshape(k_count, mode_count, W, W)
    bloch_im = bloch_sum[:, half_width:].reshape(k_count, mode_count, W, W)
    summed = jnp.sum(bloch_re * bloch_re + bloch_im * bloch_im, axis=3) / normalizer
    return summed.transpose(1, 2, 0)


def shards(g_wan, el_cells, ph_cells, q_point, kpoints, eigvec, omega):
    q_angle = angles(q_point[:, None], ph_cells)[0]
    coupling_table = coupling(q_angle, eigvec, omega)
    partial_terms = jnp.einsum(
        "pncom,epncw->emow", coupling_table, g_wan, preferred_element_type=jnp.float32
    )
    mode_vertex = lax.psum_scatter(partial_terms, "ph", scatter_dimension=1, tiled=True).astype(
        jnp.bfloat16
    )
    k_angle = angles(kpoints, el_cells)
    phase_cos = jnp.cos(k_angle).astype(jnp.bfloat16)
    phase_sin = jnp.sin(k_angle).astype(jnp.bfloat16)
    phase_left = jnp.concatenate([phase_cos, phase_sin], 1)
    cell_total = el_cells.shape[1]
    normalizer = float(cell_total * g_wan.shape[1] * lax.axis_size("ph") * W)
    results = []
    for offset in range(0, mode_vertex.shape[1], 4):
        mode_block = mode_vertex[:, offset : offset + 4]
        gathered = lax.all_gather(mode_block, "ka", axis=0, tiled=True)
        bloch_sum = jnp.dot(phase_left, stacked(gathered), preferred_element_type=jnp.float32)
        results.append(pair_strength(bloch_sum, 4, normalizer))
    return jnp.concatenate(results, 0)


def solution(mesh):
    return jax.shard_map(
        shards,
        mesh=mesh,
        in_specs=(
            P("ka", "ph", None, None, None),
            P(),
            P(None, "ph"),
            P(),
            P(None, "ka"),
            P(),
            P(),
        ),
        out_specs=P("ph", None, "ka"),
        check_vma=False,
    )
```

profile of v0, /device:TPU:0, one launch (start us, length us, event | category | flops | bytes accessed | tf_op | source)
XLA Modules:
  0.0 180.9 jit_solution(17569976806499803198)
XLA Ops:
  0.0 0.8 slice_bitcast_fusion.1
  0.9 0.8 multiply_reduce_fusion.1
  1.8 0.7 multiply_rsqrt_fusion
  2.5 0.2 multiply_convert_fusion
  2.7 0.1 fusion.45
  2.8 0.1 maximum_bitcast_fusion.2
  3.0 7.1 %fusion.6 = f32[4,48,2,1024]{3,1,0,2:T(8,128)S(1)} fusion(bf16[4,12,48,2,1024]{4,3,2,1,0:T(2,128)(2,1)} %param.7, bf16[12,48,1,2,48]{1,4,0,2,3:T(8,128)(2,1)S(1)} %get-tuple-element.17, bf16[12,48,1,2,48]{1,4,0,2,3:T(8,128)(2,1)S(1)} %get-tuple-element.16), kind=kOutput, calls=%fused_computation.15 | convolution fusion | flops 906412032 | bytes 11231232 | tf_op jit(solution)/shard_map/pncom,epncw->emow/dot_general | solution.py:49
  10.2 1.0 copy.56
  11.2 34.3 %all-reduce.2 = bf16[4,48,2,1024]{3,0,2,1:T(4,128)(2,1)S(1)} all-reduce(f32[4,48,2,1024]{3,0,2,1:T(4,128)S(1)} %copy.56), channel_id=2, replica_groups=mesh['ph'=4,'ka'=8] {'ph'}, use_global_device_ids=true, to_apply=%region_2.3.clone | all-reduce | flops 393216 | bytes 2359296
  45.5 0.6 dynamic-slice
  46.8 0.1 dynamic-slice_convert_fusion
  47.0 31.9 %all_gather.10 = bf16[32,4,2,1024]{3,1,2,0:T(4,128)(2,1)S(1)} all-gather(bf16[4,4,2,1024]{3,1,2,0:T(4,128)(2,1)S(1)} %copy.59), channel_id=1, replica_groups=mesh['ph'=4,'ka'=8] {'ka'}, dimensions={0}, use_global_device_ids=true | all-gather | bytes 589824 | tf_op jit(solution)/shard_map/all_gather | solution.py:64
  78.9 0.2 fusion.49
  79.1 0.1 copy.68
  79.4 0.1 cosine_convert_fusion
  79.6 1.3 fusion.17
  80.8 2.6 %fusion.4 = f32[256,4096]{1,0:T(8,128)} fusion(f32[256,8192]{1,0:T(8,128)S(1)} %fusion.17), kind=kLoop, calls=%fused_computation.7 | loop fusion | flops 3145728 | bytes 12582912 | tf_op jit(solution)/shard_map/add | solution.py:42
  83.4 5.6 %copy.60 = f32[256,4096]{0,1:T(8,128)} copy(f32[256,4096]{1,0:T(8,128)} %fusion.4) | data formatting | bytes 8388608 | tf_op jit(solution)/shard_map/add | solution.py:42
  89.0 2.9 %bitcast_reduce_fusion.1 = f32[256,4,32]{0,2,1:T(8,128)S(1)} fusion(f32[256,4096]{0,1:T(8,128)} %copy.60), kind=kLoop, calls=%fused_computation.13 | loop fusion | flops 1015808 | bytes 4325376 | tf_op jit(solution)/shard_map/reduce_sum | solution.py:42
  92.0 31.4 %all_gather.11 = bf16[32,4,2,1024]{3,1,2,0:T(4,128)(2,1)S(1)} all-gather(bf16[4,4,2,1024]{3,1,2,0:T(4,128)(2,1)S(1)} %copy.61), channel_id=1, replica_groups=mesh['ph'=4,'ka'=8] {'ka'}, dimensions={0}, use_global_device_ids=true | all-gather | bytes 589824 | tf_op jit(solution)/shard_map/all_gather | solution.py:64
  123.3 0.2 fusion.50
  123.7 1.3 fusion.25
  125.0 2.6 %fusion.3 = f32[256,4096]{1,0:T(8,128)} fusion(f32[256,8192]{1,0:T(8,128)S(1)} %fusion.25), kind=kLoop, calls=%fused_computation.4 | loop fusion | flops 3145728 | bytes 12582912 | tf_op jit(solution)/shard_map/add | solution.py:42
  127.6 5.6 %copy.62 = f32[256,4096]{0,1:T(8,128)} copy(f32[256,4096]{1,0:T(8,128)} %fusion.3) | data formatting | bytes 8388608 | tf_op jit(solution)/shard_map/add | solution.py:42
  133.2 2.9 %bitcast_reduce_fusion = f32[256,4,32]{0,2,1:T(8,128)S(1)} fusion(f32[256,4096]{0,1:T(8,128)} %copy.62), kind=kLoop, calls=%fused_computation.12 | loop fusion | flops 1015808 | bytes 4325376 | tf_op jit(solution)/shard_map/reduce_sum | solution.py:42
  136.2 31.2 %all_gather.9 = bf16[32,4,2,1024]{3,1,2,0:T(4,128)(2,1)S(1)} all-gather(bf16[4,4,2,1024]{3,1,2,0:T(4,128)(2,1)S(1)} %copy.57), channel_id=1, replica_groups=mesh['ph'=4,'ka'=8] {'ka'}, dimensions={0}, use_global_device_ids=true | all-gather | bytes 589824 | tf_op jit(solution)/shard_map/all_gather | solution.py:64
  167.4 0.2 fusion.48
  167.8 1.3 fusion.9
  169.1 2.6 %fusion.5 = f32[256,4096]{1,0:T(8,128)} fusion(f32[256,8192]{1,0:T(8,128)S(1)} %fusion.9), kind=kLoop, calls=%fused_computation.10 | loop fusion | flops 3145728 | bytes 12582912 | tf_op jit(solution)/shard_map/add | solution.py:42
  171.6 5.6 %copy.58 = f32[256,4096]{0,1:T(8,128)} copy(f32[256,4096]{1,0:T(8,128)} %fusion.5) | data formatting | bytes 8388608 | tf_op jit(solution)/shard_map/add | solution.py:42
  177.2 2.9 %bitcast_reduce_fusion.2 = f32[256,4,32]{0,2,1:T(8,128)S(1)} fusion(f32[256,4096]{0,1:T(8,128)} %copy.58), kind=kLoop, calls=%fused_computation.14 | loop fusion | flops 1015808 | bytes 4325376 | tf_op jit(solution)/shard_map/reduce_sum | solution.py:42
  180.1 0.8 pad_maximum_fusion
  (25 shorter events, 1.2 us)
Async XLA Ops:
  10.1 35.4 %copy-start.2 = (u32[32]{0:T(128)S(1)}, u32[32]{0:T(128)}, u32[]{:S(2)}) copy-start(u32[32]{0:T(128)} %constant.40) | copy-start | bytes 388
  10.1 69.2 %copy-start = (s32[3,256]{1,0:T(4,128)S(1)}, s32[3,256]{1,0:T(4,128)}, u32[]{:S(2)}) copy-start(s32[3,256]{1,0:T(4,128)} %param.11) | copy-start | bytes 9220
  10.2 69.2 %copy-start.1 = (s32[3,32]{1,0:T(4,128)S(1)}, s32[3,32]{1,0:T(4,128)}, u32[]{:S(2)}) copy-start(s32[3,32]{1,0:T(4,128)} %param.8) | copy-start | bytes 1156
where the time goes:
time: 182 us; the launch traced here: 181 us
  blocking collectives  129 us (71%)
  local copies, waits for them, and re-layouts  20.7 us (11%)
  other arithmetic  19.5 us (11%)
  matrix products  11 us (6%)
    all_gather x3, blocking collectives, shards(): gathered = lax.all_gather(mode_block, 'ka', axis=0, tiled=True)  94.4 us
    unnamed x1, blocking collectives  34.3 us
    add x3, local copies, waits for them, and re-layouts, pair_strength(): bloch_re * bloch_re + bloch_im * bloch_im  16.8 us
    reduce_sum x3, other arithmetic, pair_strength(): jnp.sum(bloch_re * bloch_re + bloch_im * bloch_im, axis=3) / normalizer  8.62 us
    add x3, other arithmetic, pair_strength(): bloch_re * bloch_re + bloch_im * bloch_im  7.73 us
    dot_general x1, matrix products, shards(): jnp.einsum('pncom,epncw->emow', coupling_table, g_wan, preferred_element_...  7.15 us
    dot_general x3, matrix products, shards(): jnp.dot(phase_left, stacked(gathered), preferred_element_type=jnp.float32)  3.82 us

commit v1 on v0

v1 whole, which is shorter than its diff:
```python
import functools
import math

import jax
import jax.numpy as jnp
from jax import lax
from jax.experimental import pallas as pl
from jax.experimental.pallas import tpu as pltpu
from jax.sharding import PartitionSpec as P

W = 32
KGRID = 64
MESH = pl.DeviceIdType.MESH


def angles(numerators, vectors):
    summed = jnp.sum(numerators[:, :, None] * vectors[:, None, :], axis=0)
    return jnp.mod(summed, KGRID).astype(jnp.float32) * (2.0 * math.pi / KGRID)


def splits(ways, width):
    by_width = math.gcd(ways, width // W)
    return by_width, ways // by_width


def coupling(q_angle, eigvec, omega, owners):
    mode_scale = 1.0 / jnp.sqrt(2.0 * omega)
    cos_phase = jnp.cos(q_angle)[:, None, None]
    sin_phase = jnp.sin(q_angle)[:, None, None]
    real_part = eigvec[0][None]
    imag_part = eigvec[1][None]
    coef_re = ((cos_phase * real_part - sin_phase * imag_part) * mode_scale).astype(jnp.bfloat16)
    coef_im = ((sin_phase * real_part + cos_phase * imag_part) * mode_scale).astype(jnp.bfloat16)
    table = jnp.stack([jnp.stack([coef_re, coef_im], 2), jnp.stack([-coef_im, coef_re], 2)], 2)
    cells, disp = table.shape[:2]
    return table.reshape(cells, disp, 2, 2, owners, -1).transpose(0, 1, 2, 4, 3, 5)


def kernel(
    nph, nka, part_ref, kpt_ref, cell_ref, out_ref,
    core_send, core_recv, x_send, x_recv, mine, vert_send, vert_recv, vert_f32, turned,
    k_mine, k_all, cos_re, cos_im, str_send, str_recv,
    core_ss, core_rs, x_ss, x_rs, v_ss, v_rs, k_ss, k_rs, s_ss, s_rs,
):
    ph, ka = lax.axis_index("ph"), lax.axis_index("ka")
    nx = nph // 2
    core, x = lax.rem(ph, 2), lax.div(ph, 2)
    mate = 2 * x + (1 - core)
    cells, rows_all, width = part_ref.shape
    rows = rows_all // nph
    wsplit, msplit = splits(nka, width)
    grouped = rows // msplit
    modes = grouped // 2
    wblk = width // wsplit
    block_rows = cells * grouped
    nloc = wblk // W
    kdev = kpt_ref.shape[1]
    all_cells = cell_ref.shape[0]

    barrier = pltpu.get_barrier_semaphore()
    pl.semaphore_signal(barrier, inc=1, device_id=(mate, ka), device_id_type=MESH)
    for step in range(1, nx):
        there = 2 * lax.rem(x + step, nx) + core
        pl.semaphore_signal(barrier, inc=1, device_id=(there, ka), device_id_type=MESH)
    for step in range(1, nka):
        there = lax.rem(ka + step, nka)
        pl.semaphore_signal(barrier, inc=1, device_id=(ph, there), device_id_type=MESH)

    for step in range(nx):
        owner = 2 * lax.rem(x + step, nx) + (1 - core)
        for cell in range(cells):
            block = part_ref[cell, pl.ds(pl.multiple_of(owner * rows, 8), rows), :]
            for group in range(msplit):
                at = group * block_rows + cell * grouped
                mine[at : at + grouped, :] = block[group * grouped : (group + 1) * grouped]
        core_send[step] = mine[...].astype(jnp.bfloat16)
    k_mine[...] = jnp.zeros_like(k_mine)
    k_mine[0:3, :] = kpt_ref[...]
    pl.semaphore_wait(barrier, nx + nka - 1)

    core_copies = []
    for step in range(nx - 1, -1, -1):
        copy = pltpu.make_async_remote_copy(
            src_ref=core_send.at[step], dst_ref=core_recv.at[step],
            send_sem=core_ss.at[step], recv_sem=core_rs.at[step],
            device_id=(mate, ka), device_id_type=MESH,
        )
        copy.start()
        core_copies.append((step, copy))
    k_copies = []
    for step in range(1, nka):
        there = lax.rem(ka + step, nka)
        copy = pltpu.make_async_remote_copy(
            src_ref=k_mine, dst_ref=k_all.at[ka],
            send_sem=k_ss.at[step], recv_sem=k_rs.at[ka],
            device_id=(ph, there), device_id_type=MESH,
        )
        copy.start()
        k_copies.append(copy)
    k_all[ka] = k_mine[...]

    x_copies = []
    for step, copy in core_copies:
        owner = 2 * lax.rem(x + step, nx) + core
        for cell in range(cells):
            block = part_ref[cell, pl.ds(pl.multiple_of(owner * rows, 8), rows), :]
            for group in range(msplit):
                at = group * block_rows + cell * grouped
                mine[at : at + grouped, :] = block[group * grouped : (group + 1) * grouped]
        copy.wait_recv()
        mine[...] += core_recv[step].astype(jnp.float32)
        if step > 0:
            x_send[step - 1] = mine[...].astype(jnp.bfloat16)
            send = pltpu.make_async_remote_copy(
                src_ref=x_send.at[step - 1], dst_ref=x_recv.at[step - 1],
                send_sem=x_ss.at[step - 1], recv_sem=x_rs.at[step - 1],
                device_id=(owner, ka), device_id_type=MESH,
            )
            send.start()
            x_copies.append((step, send))

    for step in range(nka):
        src = lax.rem(ka + step, nka)
        if step:
            pltpu.make_async_remote_copy(
                src_ref=k_mine, dst_ref=k_all.at[src],
                send_sem=k_ss.at[step], recv_sem=k_rs.at[src],
                device_id=(ph, src), device_id_type=MESH,
            ).wait_recv()
    def phases(src, carry):
        numer = k_all[src]
        summed = (
            cell_ref[:, 0:1] * numer[0:1, :]
            + cell_ref[:, 1:2] * numer[1:2, :]
            + cell_ref[:, 2:3] * numer[2:3, :]
        )
        angle = jnp.bitwise_and(summed, KGRID - 1).astype(jnp.float32) * (2.0 * math.pi / KGRID)
        cosine, sine = jnp.cos(angle), jnp.sin(angle)
        cos_re[src] = jnp.concatenate([cosine, -sine], 0).astype(jnp.bfloat16)
        cos_im[src] = jnp.concatenate([sine, cosine], 0).astype(jnp.bfloat16)
        return carry

    lax.fori_loop(0, nka, phases, 0)

    for step, send in x_copies:
        send.wait_recv()
        mine[...] += x_recv[step - 1].astype(jnp.float32)

    for step in range(nka):
        group, part = divmod(step, wsplit)
        vert_send[step] = mine[
            group * block_rows : (group + 1) * block_rows, part * wblk : (part + 1) * wblk
        ].astype(jnp.bfloat16)
    v_copies = []
    for step in range(1, nka):
        there = lax.rem(ka + step, nka)
        copy = pltpu.make_async_remote_copy(
            src_ref=vert_send.at[there], dst_ref=vert_recv.at[ka],
            send_sem=v_ss.at[step], recv_sem=v_rs.at[ka],
            device_id=(ph, there), device_id_type=MESH,
        )
        copy.start()
        v_copies.append(copy)
    vert_recv[ka] = vert_send[ka]
    for step in range(1, nka):
        src = lax.rem(ka + step, nka)
        pltpu.make_async_remote_copy(
            src_ref=vert_send.at[src], dst_ref=vert_recv.at[src],
            send_sem=v_ss.at[step], recv_sem=v_rs.at[src],
            device_id=(ph, src), device_id_type=MESH,
        ).wait_recv()
    for src in range(nka):
        vert_f32[src * block_rows : (src + 1) * block_rows, :] = vert_recv[src].astype(jnp.float32)
    for mode in range(modes):
        real = vert_f32[pl.ds(mode, all_cells, stride=grouped), :]
        imag = vert_f32[pl.ds(modes + mode, all_cells, stride=grouped), :]
        turned[mode] = jnp.concatenate([real, imag], 0).T.astype(jnp.bfloat16)

    def strengths(step, carry):
        there = lax.rem(ka + step + 1, nka)
        phase_re, phase_im = cos_re[there], cos_im[there]
        for mode in range(modes):
            left = turned[mode]
            bloch_re = jnp.dot(left, phase_re, preferred_element_type=jnp.float32)
            bloch_im = jnp.dot(left, phase_im, preferred_element_type=jnp.float32)
            squares = bloch_re * bloch_re + bloch_im * bloch_im
            str_send[there, mode * nloc : (mode + 1) * nloc, :] = jnp.sum(
                squares.reshape(nloc, W, kdev), axis=1
            )

        @pl.when(step < nka - 1)
        def _():
            pltpu.make_async_remote_copy(
                src_ref=str_send.at[there], dst_ref=str_recv.at[ka],
                send_sem=s_ss.at[there], recv_sem=s_rs.at[ka],
                device_id=(ph, there), device_id_type=MESH,
            ).start()

        return carry

    lax.fori_loop(0, nka, strengths, 0)
    str_recv[ka] = str_send[ka]
    for step in range(1, nka):
        src = lax.rem(ka + step, nka)
        pltpu.make_async_remote_copy(
            src_ref=str_send.at[src], dst_ref=str_recv.at[src],
            send_sem=s_ss.at[src], recv_sem=s_rs.at[src],
            device_id=(ph, src), device_id_type=MESH,
        ).wait()
    for src in range(nka):
        for mode in range(modes):
            group, part = divmod(src, wsplit)
            out_ref[group * modes + mode, part * nloc : (part + 1) * nloc, :] = str_recv[
                src, mode * nloc : (mode + 1) * nloc, :
            ]
    for step, copy in core_copies:
        copy.wait_send()
    for step, copy in x_copies:
        copy.wait_send()
    for copy in k_copies + v_copies:
        copy.wait_send()


def shards(g_wan, el_cells, ph_cells, q_point, kpoints, eigvec, omega):
    nph, nka = lax.axis_size("ph"), lax.axis_size("ka")
    q_angle = angles(q_point[:, None], ph_cells)[0]
    wsplit, msplit = splits(nka, g_wan.shape[-1])
    table = coupling(q_angle, eigvec, omega, nph * msplit)
    partial_terms = jnp.einsum(
        "pncqom,epncw->eqomw", table, g_wan, preferred_element_type=jnp.float32
    )
    cells, width = g_wan.shape[0], g_wan.shape[-1]
    mode_total = eigvec.shape[-1]
    modes = mode_total // nph
    partial_terms = partial_terms.reshape(cells, 2 * mode_total, width)
    kdev, all_cells = kpoints.shape[1], el_cells.shape[1]
    nx, wblk = nph // 2, width // wsplit
    nloc = wblk // W
    rows = cells * 2 * modes
    grouped = modes // msplit
    block_rows = cells * 2 * grouped
    bf16, f32 = jnp.bfloat16, jnp.float32
    vmem, dma = pltpu.VMEM, pltpu.SemaphoreType.DMA
    summed = pl.pallas_call(
        functools.partial(kernel, nph, nka),
        out_shape=jax.ShapeDtypeStruct((modes, W, kdev), f32),
        in_specs=[pl.BlockSpec(memory_space=vmem)] * 3,
        out_specs=pl.BlockSpec(memory_space=vmem),
        scratch_shapes=[
            vmem((nx, rows, width), bf16),
            vmem((nx, rows, width), bf16),
            vmem((nx - 1, rows, width), bf16),
            vmem((nx - 1, rows, width), bf16),
            vmem((rows, width), f32),
            vmem((nka, block_rows, wblk), bf16),
            vmem((nka, block_rows, wblk), bf16),
            vmem((nka * block_rows, wblk), f32),
            vmem((grouped, wblk, 2 * all_cells), bf16),
            vmem((8, kdev), jnp.int32),
            vmem((nka, 8, kdev), jnp.int32),
            vmem((nka, 2 * all_cells, kdev), bf16),
            vmem((nka, 2 * all_cells, kdev), bf16),
            vmem((nka, grouped * nloc, kdev), f32),
            vmem((nka, grouped * nloc, kdev), f32),
            dma((nx,)), dma((nx,)), dma((nx - 1,)), dma((nx - 1,)),
            dma((nka,)), dma((nka,)), dma((nka,)), dma((nka,)), dma((nka,)), dma((nka,)),
        ],
        compiler_params=pltpu.CompilerParams(
            collective_id=0, has_side_effects=True, vmem_limit_bytes=56 * 1024 * 1024
        ),
    )(partial_terms, kpoints, el_cells.T)
    normalizer = float(all_cells * g_wan.shape[1] * nph * W)
    return summed / normalizer


def solution(mesh):
    return jax.shard_map(
        shards,
        mesh=mesh,
        in_specs=(
            P("ka", "ph", None, None, None),
            P(),
            P(None, "ph"),
            P(),
            P(None, "ka"),
            P(),
            P(),
        ),
        out_specs=P("ph", None, "ka"),
        check_vma=False,
    )
```

time: 182 us -> 47.8 us (0.26)
  blocking collectives: 129 us -> 0 us
  Pallas kernels: 0 us -> 31.5 us
  local copies, waits for them, and re-layouts: 20.7 us -> 4.83 us
  other arithmetic: 19.5 us -> 3.74 us
  matrix products: 11 us -> 7.32 us
    all_gather x3 -> x0, blocking collectives: 94.4 us -> none  [shards(): gathered = lax.all_gather(mode_block, 'ka', axis=0, tiled=True)]
    unnamed x1 -> x0, blocking collectives: 34.3 us -> none
    pallas_call x0 -> x1, Pallas kernels: none -> 31.5 us  [shards(): pl.pallas_call(functools.partial(kernel, nph, nka), out_shape=jax.ShapeDt...]
    add x3 -> x0, local copies, waits for them, and re-layouts: 16.8 us -> none  [pair_strength(): bloch_re * bloch_re + bloch_im * bloch_im]
    reduce_sum x3 -> x0, other arithmetic: 8.62 us -> none  [pair_strength(): jnp.sum(bloch_re * bloch_re + bloch_im * bloch_im, axis=3) / normalizer]
    add x3 -> x0, other arithmetic: 7.73 us -> none  [pair_strength(): bloch_re * bloch_re + bloch_im * bloch_im]
    dot_general x4 -> x1, matrix products: 11 us -> 7.32 us  [shards(): jnp.einsum('pncqom,epncw->eqomw', table, g_wan, preferred_element_type=jn...]
    reshape x0 -> x1, local copies, waits for them, and re-layouts: none -> 2.07 us  [shards(): partial_terms = partial_terms.reshape(cells, 2 * mode_total, width)]
where the time goes in v1:
time: 47.8 us; the launch traced here: 47.5 us
  Pallas kernels  31.5 us (66%)
  matrix products  7.32 us (15%)
  local copies, waits for them, and re-layouts  4.83 us (10%)
  other arithmetic  3.74 us (8%)
    pallas_call x1, Pallas kernels, shards(): pl.pallas_call(functools.partial(kernel, nph, nka), out_shape=jax.ShapeDt...  31.5 us
    dot_general x1, matrix products, shards(): jnp.einsum('pncqom,epncw->eqomw', table, g_wan, preferred_element_type=jn...  7.32 us
    reshape x1, local copies, waits for them, and re-layouts, shards(): partial_terms = partial_terms.reshape(cells, 2 * mode_total, width)  2.07 us
    div x1, other arithmetic, shards(): return summed / normalizer  1.78 us
    transpose x1, local copies, waits for them, and re-layouts, shards(): jnp.einsum('pncqom,epncw->eqomw', table, g_wan, preferred_element_type=jn...  1.02 us

profile of v1, /device:TPU:0, one launch (start us, length us, event | category | flops | bytes accessed | tf_op | source)
XLA Modules:
  0.0 47.5 jit_solution(12955209137621462982)
XLA Ops:
  0.0 0.8 %fusion.18 = (f32[1,48,48]{2,1,0:T(8,128)S(1)}, f32[1,48,48]{2,1,0:T(8,128)S(1)}) fusion(f32[2,48,48]{2,1,0:T(8,128)} %param.12), kind=kLoop, calls=%fused_computation.24 | loop fusion | bytes 36864 | tf_op jit(solution)/shard_map/slice | solution.py:30
  0.8 0.1 copy.13
  0.8 0.1 copy.14
  0.9 0.8 %multiply_reduce_fusion = s32[12]{0:T(128)S(1)} fusion(s32[3,12]{1,0:T(4,128)} %param.9, s32[3]{0:T(128)} %param.10), kind=kLoop, calls=%fused_computation.15 | loop fusion | flops 60 | bytes 204 | tf_op jit(solution)/shard_map/reduce_sum | solution.py:17
  1.7 0.1 fusion.16
  1.8 0.7 %multiply_rsqrt_fusion = f32[48]{0:T(128)S(1)} fusion(f32[48]{0:T(128)} %param.13), kind=kLoop, calls=%fused_computation.20 | loop fusion | flops 48 | bytes 384 | tf_op jit(solution)/shard_map/sqrt | solution.py:27
  2.5 0.1 mul.171
  2.5 0.3 multiply_convert_fusion
  2.9 0.2 fusion.15
  3.0 7.3 %fusion.2 = f32[4,4,2,12,1024]{4,3,0,2,1:T(8,128)S(1)} fusion(bf16[4,12,48,2,1024,1,1]{4,3,2,1,0,6,5:T(2,128)(2,1)} %bitcast.22, bf16[12,48,1,1,4,12]{1,5,0,2,3,4:T(8,128)(2,1)S(1)} %get-tuple-element.8, bf16[12,48,1,1,4,12]{1,5,0,2,3,4:T(8,128)(2,1)S(1)} %fusion.15, bf16[12,48,1,1,4,12]{1,5,0,2,3,4:T(8,128)(2,1)S(1)} %get-tuple-element.7), kind=kOutput, calls=%fused_computation.2 | convolution fusion | flops 906854400 | bytes 11175936 | tf_op jit(solution)/shard_map/pncqom,epncw->eqomw/dot_general | solution.py:229
  10.4 1.0 %copy.16 = f32[4,4,2,12,1024]{4,0,3,2,1:T(4,128)S(1)} copy(f32[4,4,2,12,1024]{4,3,0,2,1:T(8,128)S(1)} %fusion.2) | data formatting | bytes 3145728 | tf_op jit(solution)/shard_map/pncqom,epncw->eqomw/transpose | solution.py:229
  11.4 0.0 copy-start
  11.4 2.1 %copy.18.part_ref = f32[4,96,1024]{2,1,0:T(8,128)} copy(f32[4,96,1024]{2,0,1:T(4,128)S(1)} %bitcast.20) | data formatting | bytes 3145728 | tf_op jit(solution)/shard_map/reshape | solution.py:235
  13.5 0.0 copy-done
  13.5 0.7 %copy.17 = s32[3,32]{0,1:T(8,128)} copy(s32[3,32]{1,0:T(4,128)S(1)} %copy-done) | data formatting | bytes 768 | tf_op args[1]
  14.2 31.5 %shard_map.73 = f32[12,32,256]{2,1,0:T(8,128)} custom-call(f32[4,96,1024]{2,1,0:T(8,128)} %copy.18.part_ref, s32[3,256]{1,0:T(4,128)} %kpt_ref.1, s32[32,3]{1,0:T(8,128)} %bitcast.21), custom_call_target="tpu_custom_call" | custom-call | tf_op jit(solution)/shard_map/pallas_call | solution.py:244
  45.7 1.8 %broadcast_multiply_fusion = f32[12,32,256]{2,1,0:T(8,128)} fusion(f32[12,32,256]{2,1,0:T(8,128)} %shard_map.73), kind=kLoop, calls=%fused_computation.12 | loop fusion | flops 98304 | bytes 786432 | tf_op jit(solution)/shard_map/div | solution.py:273
  (3 shorter events, 0.1 us)
Async XLA Ops:
  11.4 2.1 %copy-start = (s32[3,32]{1,0:T(4,128)S(1)}, s32[3,32]{1,0:T(4,128)}, u32[]{:S(2)}) copy-start(s32[3,32]{1,0:T(4,128)} %param.8) | copy-start | bytes 1156

commit v2 on v1

v2 whole, which is shorter than its diff:
```python
import functools
import math

import jax
import jax.numpy as jnp
from jax import lax
from jax.experimental import pallas as pl
from jax.experimental.pallas import tpu as pltpu
from jax.sharding import PartitionSpec as P

W = 32
KGRID = 64
LANES = 128
MESH = pl.DeviceIdType.MESH


def splits(ways, width):
    by_width = math.gcd(ways, width // W)
    return by_width, ways // by_width


def cell_groups(cells, grouped):
    return 2 if cells % 2 == 0 and (cells // 2 * grouped) % 16 == 0 else 1


def turn(numerator):
    folded = numerator - KGRID * jnp.floor(numerator * (1.0 / KGRID))
    return folded * (2.0 * math.pi / KGRID)


def kernel(
    nph, nka, normalizer, g_ref, kpt_ref, cell_ref, q_ref, phc_ref, eig_ref, omega_ref, out_ref,
    g_buf, table, part, core_send, core_recv, x_send, x_recv, vert_send, vert_recv, vert_f32, turned,
    k_mine, k_all, cos_re, cos_im, str_send, str_recv,
    g_sem, core_ss, core_rs, x_ss, x_rs, v_ss, v_rs, k_ss, k_rs, s_ss, s_rs,
):
    ph, ka = lax.axis_index("ph"), lax.axis_index("ka")
    nx = nph // 2
    core, x = lax.rem(ph, 2), lax.div(ph, 2)
    mate = 2 * x + (1 - core)
    cells, pairs, tiles = g_ref.shape[:3]
    depth = 2 * pairs
    width = tiles * LANES
    rows_all = part.shape[1]
    rows = rows_all // nph
    wsplit, msplit = splits(nka, width)
    grouped = rows // msplit
    modes = grouped // 2
    wblk = width // wsplit
    nloc = wblk // W
    block_rows = cells * grouped
    groups = cell_groups(cells, grouped)
    group_cells = cells // groups
    group_rows = group_cells * grouped
    halves = 2
    half = width // halves
    kdev = kpt_ref.shape[1]
    all_cells = cell_ref.shape[1]
    mode_total = omega_ref.shape[1]
    disp = eig_ref.shape[1]

    chunks = [(g, h) for g in range(groups) for h in range(halves)]
    tiles_half = tiles // halves
    g_copies = {}
    for g, h in chunks:
        for cell in range(g * group_cells, (g + 1) * group_cells):
            for tile in range(h * tiles_half, (h + 1) * tiles_half):
                copy = pltpu.make_async_copy(
                    g_ref.at[cell, :, tile], g_buf.at[cell, tile], g_sem.at[cell, tile]
                )
                copy.start()
                g_copies[cell, tile] = copy

    barrier = pltpu.get_barrier_semaphore()
    pl.semaphore_signal(barrier, inc=1, device_id=(mate, ka), device_id_type=MESH)
    for step in range(1, nx):
        there = 2 * lax.rem(x + step, nx) + core
        pl.semaphore_signal(barrier, inc=1, device_id=(there, ka), device_id_type=MESH)
    for step in range(1, nka):
        there = lax.rem(ka + step, nka)
        pl.semaphore_signal(barrier, inc=1, device_id=(ph, there), device_id_type=MESH)

    spread_v = lax.broadcasted_iota(jnp.int32, (disp, 2 * disp), 0)
    spread_col = lax.broadcasted_iota(jnp.int32, (disp, 2 * disp), 1)
    even = (spread_col == 2 * spread_v).astype(jnp.float32)
    odd = (spread_col == 2 * spread_v + 1).astype(jnp.float32)

    def spread(values, pattern):
        return lax.dot_general(
            values, pattern, (((0,), (0,)), ((), ())),
            preferred_element_type=jnp.float32, precision=lax.Precision.HIGHEST,
        )

    real, imag = eig_ref[0], eig_ref[1]
    first = spread(real, even) - spread(imag, odd)
    second = spread(imag, even) + spread(real, odd)

    def by_owner(upper, lower):
        pieces = []
        for at in range(0, mode_total, modes):
            pieces += [upper[at : at + modes], lower[at : at + modes]]
        return jnp.concatenate(pieces, 0)

    scale = 1.0 / jnp.sqrt(2.0 * jnp.broadcast_to(omega_ref[...], (2 * disp, mode_total)).T)
    scale = by_owner(scale, scale)
    with_cos = by_owner(first, second)
    with_sin = by_owner(-second, first)
    numer = (
        q_ref[0] * phc_ref[0:1, :] + q_ref[1] * phc_ref[1:2, :] + q_ref[2] * phc_ref[2:3, :]
    )
    q_angle = jnp.bitwise_and(numer, KGRID - 1).astype(jnp.float32) * (2.0 * math.pi / KGRID)
    q_cos, q_sin = jnp.cos(q_angle), jnp.sin(q_angle)
    pieces = []
    for p in range(phc_ref.shape[1]):
        pieces.append(
            (with_cos * q_cos[:, p : p + 1] + with_sin * q_sin[:, p : p + 1]) * scale
        )
    table[...] = jnp.concatenate(pieces, 1).astype(jnp.bfloat16)

    k_mine[...] = jnp.zeros_like(k_mine)
    k_mine[0:3, :] = kpt_ref[...].astype(jnp.float32)
    pl.semaphore_wait(barrier, nx + nka - 1)
    k_copies = []
    for step in range(1, nka):
        there = lax.rem(ka + step, nka)
        copy = pltpu.make_async_remote_copy(
            src_ref=k_mine, dst_ref=k_all.at[ka],
            send_sem=k_ss.at[step], recv_sem=k_rs.at[ka],
            device_id=(ph, there), device_id_type=MESH,
        )
        copy.start()
        k_copies.append(copy)
    k_all[ka] = k_mine[...]

    def owned(owner, index):
        g, h = chunks[index]
        blocks = [
            part[cell, pl.ds(pl.multiple_of(owner * rows, 8), rows), h * half : (h + 1) * half]
            for cell in range(g * group_cells, (g + 1) * group_cells)
        ]
        return jnp.concatenate(
            [
                block[group * grouped : (group + 1) * grouped]
                for group in range(msplit)
                for block in blocks
            ],
            0,
        )

    def multiply(index):
        g, h = chunks[index]
        for cell in range(g * group_cells, (g + 1) * group_cells):
            for tile in range(h * tiles_half, (h + 1) * tiles_half, 2):
                g_copies[cell, tile].wait()
                g_copies[cell, tile + 1].wait()
                right = jnp.concatenate(
                    [
                        g_buf[cell, tile].reshape(depth, LANES),
                        g_buf[cell, tile + 1].reshape(depth, LANES),
                    ],
                    1,
                )
                part[cell, :, tile * LANES : (tile + 2) * LANES] = jnp.dot(
                    table[...], right, preferred_element_type=jnp.float32
                )

    core_copies, x_copies, v_copies = {}, {}, []

    def to_mate(index):
        for step in range(nx - 1, -1, -1):
            owner = 2 * lax.rem(x + step, nx) + (1 - core)
            core_send[index, step] = owned(owner, index).astype(jnp.bfloat16)
            copy = pltpu.make_async_remote_copy(
                src_ref=core_send.at[index, step], dst_ref=core_recv.at[index, step],
                send_sem=core_ss.at[index, step], recv_sem=core_rs.at[index, step],
                device_id=(mate, ka), device_id_type=MESH,
            )
            copy.start()
            core_copies[index, step] = copy

    def to_other_chips(index):
        for step in range(1, nx):
            owner = 2 * lax.rem(x + step, nx) + core
            core_copies[index, step].wait_recv()
            both = owned(owner, index) + core_recv[index, step].astype(jnp.float32)
            x_send[index, step - 1] = both.astype(jnp.bfloat16)
            copy = pltpu.make_async_remote_copy(
                src_ref=x_send.at[index, step - 1], dst_ref=x_recv.at[index, step - 1],
                send_sem=x_ss.at[index, step - 1], recv_sem=x_rs.at[index, step - 1],
                device_id=(owner, ka), device_id_type=MESH,
            )
            copy.start()
            x_copies[index, step] = copy

    def vertices(index):
        g, h = chunks[index]
        core_copies[index, 0].wait_recv()
        total = owned(ph, index) + core_recv[index, 0].astype(jnp.float32)
        for step in range(1, nx):
            x_copies[index, step].wait_recv()
            total = total + x_recv[index, step - 1].astype(jnp.float32)
        total = total.astype(jnp.bfloat16)
        here = wsplit // halves
        for group in range(msplit):
            for local in range(here):
                vert_send[group * wsplit + h * here + local, g] = total[
                    group * group_rows : (group + 1) * group_rows,
                    local * wblk : (local + 1) * wblk,
                ]
        for group in range(msplit):
            for local in range(here):
                there = group * wsplit + h * here + lax.rem(local + ka, here)

                @pl.when(there != ka)
                def _():
                    pltpu.make_async_remote_copy(
                        src_ref=vert_send.at[there, g], dst_ref=vert_recv.at[ka, g],
                        send_sem=v_ss.at[there, g], recv_sem=v_rs.at[ka, g],
                        device_id=(ph, there), device_id_type=MESH,
                    ).start()

                @pl.when(there == ka)
                def _():
                    vert_recv[ka, g] = vert_send[there, g]

    count = len(chunks)
    for index in range(count):
        multiply(index)
        to_mate(index)
        if index >= 1:
            to_other_chips(index - 1)
        if index >= 3:
            vertices(index - 3)
    to_other_chips(count - 1)
    for index in range(max(count - 3, 0), count - 1):
        vertices(index)

    for step in range(1, nka):
        src = lax.rem(ka + step, nka)
        pltpu.make_async_remote_copy(
            src_ref=k_mine, dst_ref=k_all.at[src],
            send_sem=k_ss.at[step], recv_sem=k_rs.at[src],
            device_id=(ph, src), device_id_type=MESH,
        ).wait_recv()
    el_cells = jnp.concatenate(
        [cell_ref[...].astype(jnp.float32), jnp.zeros((5, all_cells), jnp.float32)], 0
    )

    def phases(src, carry):
        angle = turn(
            lax.dot_general(
                el_cells, k_all[src], (((0,), (0,)), ((), ())), preferred_element_type=jnp.float32
            )
        )
        cosine, sine = jnp.cos(angle), jnp.sin(angle)
        cos_re[src] = jnp.concatenate([cosine, -sine], 0).astype(jnp.bfloat16)
        cos_im[src] = jnp.concatenate([sine, cosine], 0).astype(jnp.bfloat16)
        return carry

    lax.fori_loop(0, nka, phases, 0)
    vertices(count - 1)

    for step in range(1, nka):
        src = lax.rem(ka + step, nka)
        for g in range(groups):
            pltpu.make_async_remote_copy(
                src_ref=vert_send.at[src, g], dst_ref=vert_recv.at[src, g],
                send_sem=v_ss.at[src, g], recv_sem=v_rs.at[src, g],
                device_id=(ph, src), device_id_type=MESH,
            ).wait()
    for src in range(nka):
        for g in range(groups):
            at = src * block_rows + g * group_rows
            vert_f32[at : at + group_rows, :] = vert_recv[src, g].astype(jnp.float32)
    for mode in range(modes):
        re_rows = vert_f32[pl.ds(mode, all_cells, stride=grouped), :]
        im_rows = vert_f32[pl.ds(modes + mode, all_cells, stride=grouped), :]
        turned[mode * wblk : (mode + 1) * wblk, :] = (
            jnp.concatenate([re_rows, im_rows], 0).T.astype(jnp.bfloat16)
        )

    batch = 4 if modes % 4 == 0 else 1

    def strengths(step, carry):
        there = lax.rem(ka + step + 1, nka)
        phase_re, phase_im = cos_re[there], cos_im[there]
        for mode in range(0, modes, batch):
            left = turned[mode * wblk : (mode + batch) * wblk, :]
            bloch_re = jnp.dot(left, phase_re, preferred_element_type=jnp.float32)
            bloch_im = jnp.dot(left, phase_im, preferred_element_type=jnp.float32)
            squares = bloch_re * bloch_re + bloch_im * bloch_im
            str_send[there, mode * nloc : (mode + batch) * nloc, :] = (
                jnp.sum(squares.reshape(batch * nloc, W, kdev), axis=1) / normalizer
            )

        @pl.when(step < nka - 1)
        def _():
            pltpu.make_async_remote_copy(
                src_ref=str_send.at[there], dst_ref=str_recv.at[ka],
                send_sem=s_ss.at[there], recv_sem=s_rs.at[ka],
                device_id=(ph, there), device_id_type=MESH,
            ).start()

        return carry

    lax.fori_loop(0, nka, strengths, 0)

    def place(src, held):
        group, piece = divmod(src, wsplit)
        for mode in range(modes):
            out_ref[group * modes + mode, piece * nloc : (piece + 1) * nloc, :] = held[
                src, mode * nloc : (mode + 1) * nloc, :
            ]

    str_recv[ka] = str_send[ka]
    for step in range(1, nka):
        src = lax.rem(ka + step, nka)
        pltpu.make_async_remote_copy(
            src_ref=str_send.at[src], dst_ref=str_recv.at[src],
            send_sem=s_ss.at[src], recv_sem=s_rs.at[src],
            device_id=(ph, src), device_id_type=MESH,
        ).wait()
    for src in range(nka):
        place(src, str_recv)
    for copy in list(core_copies.values()) + list(x_copies.values()) + k_copies:
        copy.wait_send()


def shards(g_wan, el_cells, ph_cells, q_point, kpoints, eigvec, omega):
    nph, nka = lax.axis_size("ph"), lax.axis_size("ka")
    cells, ph_loc, disp, parts, width = g_wan.shape
    tiles = width // LANES
    g_view = g_wan.reshape(cells, ph_loc * disp, parts, tiles, LANES).transpose(0, 1, 3, 2, 4)
    wsplit, msplit = splits(nka, width)
    mode_total = eigvec.shape[-1]
    modes = mode_total // nph
    kdev, all_cells = kpoints.shape[1], el_cells.shape[1]
    nx, wblk = nph // 2, width // wsplit
    nloc = wblk // W
    mode_group = modes // msplit
    block_rows = cells * 2 * mode_group
    groups = cell_groups(cells, 2 * mode_group)
    group_rows = block_rows // groups
    chunks = groups * 2
    sent = (chunks, nx, msplit * group_rows, width // 2)
    passed = (chunks, nx - 1, msplit * group_rows, width // 2)
    bf16, f32 = jnp.bfloat16, jnp.float32
    vmem, dma = pltpu.VMEM, pltpu.SemaphoreType.DMA
    in_vmem, in_smem = pl.BlockSpec(memory_space=vmem), pl.BlockSpec(memory_space=pltpu.SMEM)
    normalizer = float(all_cells * ph_loc * nph * W)
    return pl.pallas_call(
        functools.partial(kernel, nph, nka, normalizer),
        out_shape=jax.ShapeDtypeStruct((modes, W, kdev), f32),
        in_specs=[
            pl.BlockSpec(memory_space=pl.ANY), in_vmem, in_vmem, in_smem, in_vmem, in_vmem, in_vmem
        ],
        out_specs=in_vmem,
        scratch_shapes=[
            vmem((cells, tiles, ph_loc * disp, parts, LANES), bf16),
            vmem((2 * mode_total, ph_loc * disp * parts), bf16),
            vmem((cells, 2 * mode_total, width), f32),
            vmem(sent, bf16),
            vmem(sent, bf16),
            vmem(passed, bf16),
            vmem(passed, bf16),
            vmem((nka, groups, group_rows, wblk), bf16),
            vmem((nka, groups, group_rows, wblk), bf16),
            vmem((nka * block_rows, wblk), f32),
            vmem((mode_group * wblk, 2 * all_cells), bf16),
            vmem((8, kdev), f32),
            vmem((nka, 8, kdev), f32),
            vmem((nka, 2 * all_cells, kdev), bf16),
            vmem((nka, 2 * all_cells, kdev), bf16),
            vmem((nka, mode_group * nloc, kdev), f32),
            vmem((nka, mode_group * nloc, kdev), f32),
            dma((cells, tiles)),
            dma(sent[:2]), dma(sent[:2]), dma(passed[:2]), dma(passed[:2]),
            dma((nka, groups)), dma((nka, groups)),
            dma((nka,)), dma((nka,)), dma((nka,)), dma((nka,)),
        ],
        compiler_params=pltpu.CompilerParams(
            collective_id=0, has_side_effects=True, vmem_limit_bytes=56 * 1024 * 1024
        ),
    )(g_view, kpoints, el_cells, q_point, ph_cells, eigvec, omega.reshape(1, mode_total))


def solution(mesh):
    return jax.shard_map(
        shards,
        mesh=mesh,
        in_specs=(
            P("ka", "ph", None, None, None),
            P(),
            P(None, "ph"),
            P(),
            P(None, "ka"),
            P(),
            P(),
        ),
        out_specs=P("ph", None, "ka"),
        check_vma=False,
    )
```

time: 47.8 us -> 36.1 us (0.76)
  matrix products: 7.32 us -> 0 us
  other arithmetic: 3.74 us -> 0 us
  local copies, waits for them, and re-layouts: 4.83 us -> 1.77 us
  Pallas kernels: 31.5 us -> 34.1 us
    dot_general x1 -> x0, matrix products: 7.32 us -> none  [shards(): jnp.einsum('pncqom,epncw->eqomw', table, g_wan, preferred_element_type=jn...]
    pallas_call x1, Pallas kernels: 31.5 us -> 34.1 us  [shards(): pl.pallas_call(functools.partial(kernel, nph, nka, normalizer), out_shape...]
    reshape x1 -> x0, local copies, waits for them, and re-layouts: 2.07 us -> none  [shards(): partial_terms = partial_terms.reshape(cells, 2 * mode_total, width)]
    div x1 -> x0, other arithmetic: 1.78 us -> none  [shards(): return summed / normalizer]
    unnamed x3 -> x1, local copies, waits for them, and re-layouts: 0.7 us -> 1.77 us
    transpose x1 -> x0, local copies, waits for them, and re-layouts: 1.02 us -> none  [shards(): jnp.einsum('pncqom,epncw->eqomw', table, g_wan, preferred_element_type=jn...]
    slice x3 -> x0, local copies, waits for them, and re-layouts: 0.91 us -> none  [the longest x2 0.83 us: coupling(): real_part = eigvec[0][None]]
    reduce_sum x1 -> x0, other arithmetic: 0.77 us -> none  [angles(): summed = jnp.sum(numerators[:, :, None] * vectors[:, None, :], axis=0)]
where the time goes in v2:
time: 36.1 us; the launch traced here: 35.9 us
  Pallas kernels  34.1 us (94%)
  local copies, waits for them, and re-layouts  1.77 us (5%)
    pallas_call x1, Pallas kernels, shards(): pl.pallas_call(functools.partial(kernel, nph, nka, normalizer), out_shape...  34.1 us
    unnamed x1, local copies, waits for them, and re-layouts  1.77 us

profile of v2, /device:TPU:0, one launch (start us, length us, event | category | flops | bytes accessed | tf_op | source)
XLA Modules:
  0.0 35.9 jit_solution(17354024321077181698)
XLA Ops:
  0.0 34.1 %shard_map.73 = f32[12,32,256]{2,1,0:T(8,128)} custom-call(bf16[4,576,8,2,128]{4,3,2,1,0:T(2,128)(2,1)} %bitcast.4, s32[3,256]{1,0:T(4,128)} %kpt_ref.1, s32[3,32]{1,0:T(4,128)} %cell_ref.1, s32[3]{0:T(128)} %q_ref.1, s32[3,12]{1,0:T(4,128)} %phc_ref.1, f32[2,48,48]{2,1,0:T(8,128)} %eig_ref.1, f32[1,48]{1,0:T(1,128)} %bitcast.5), custom_call_target="tpu_custom_call" | custom-call | tf_op jit(solution)/shard_map/pallas_call | solution.py:351
  34.1 1.8 %copy.9 = f32[12,32,256]{2,1,0:T(8,128)} copy(f32[12,32,256]{2,1,0:T(8,128)} %shard_map.73) | data formatting | bytes 786432

commit v3 on v2

--- a/solution.py
+++ b/solution.py
@@ -14,6 +14,10 @@
 MESH = pl.DeviceIdType.MESH
 
 
+def team_size(nka):
+    return nka // 2 if nka % 2 == 0 else nka
+
+
 def splits(ways, width):
     by_width = math.gcd(ways, width // W)
     return by_width, ways // by_width
@@ -23,9 +27,23 @@
     return 2 if cells % 2 == 0 and (cells // 2 * grouped) % 16 == 0 else 1
 
 
-def turn(numerator):
+def cos_sin(numerator):
     folded = numerator - KGRID * jnp.floor(numerator * (1.0 / KGRID))
-    return folded * (2.0 * math.pi / KGRID)
+    quarter = jnp.floor((folded + KGRID // 8) * (4.0 / KGRID))
+    angle = (folded - quarter * (KGRID // 4)) * (2.0 * math.pi / KGRID)
+    square = angle * angle
+    cosine = 1.0 + square * (
+        -1 / 2 + square * (1 / 24 + square * (-1 / 720 + square * (1 / 40320)))
+    )
+    sine = angle + angle * square * (
+        -1 / 6 + square * (1 / 120 + square * (-1 / 5040 + square * (1 / 362880)))
+    )
+    odd = (quarter == 1.0) | (quarter == 3.0)
+    cos_minus = (quarter == 1.0) | (quarter == 2.0)
+    sin_minus = (quarter == 2.0) | (quarter == 3.0)
+    cos_all = jnp.where(odd, sine, cosine)
+    sin_all = jnp.where(odd, cosine, sine)
+    return jnp.where(cos_minus, -cos_all, cos_all), jnp.where(sin_minus, -sin_all, sin_all)
 
 
 def kernel(
@@ -43,11 +61,14 @@
     width = tiles * LANES
     rows_all = part.shape[1]
     rows = rows_all // nph
-    wsplit, msplit = splits(nka, width)
+    ways = team_size(nka)
+    team, spot = lax.div(ka, ways), lax.rem(ka, ways)
+    wsplit, msplit = splits(ways, width)
     grouped = rows // msplit
     modes = grouped // 2
     wblk = width // wsplit
     nloc = wblk // W
+    lanes = vert_f32.shape[2]
     block_rows = cells * grouped
     groups = cell_groups(cells, grouped)
     group_cells = cells // groups
@@ -108,8 +129,7 @@
     numer = (
         q_ref[0] * phc_ref[0:1, :] + q_ref[1] * phc_ref[1:2, :] + q_ref[2] * phc_ref[2:3, :]
     )
-    q_angle = jnp.bitwise_and(numer, KGRID - 1).astype(jnp.float32) * (2.0 * math.pi / KGRID)
-    q_cos, q_sin = jnp.cos(q_angle), jnp.sin(q_angle)
+    q_cos, q_sin = cos_sin(numer.astype(jnp.float32))
     pieces = []
     for p in range(phc_ref.shape[1]):
         pieces.append(
@@ -121,16 +141,16 @@
     k_mine[0:3, :] = kpt_ref[...].astype(jnp.float32)
     pl.semaphore_wait(barrier, nx + nka - 1)
     k_copies = []
-    for step in range(1, nka):
-        there = lax.rem(ka + step, nka)
+    for step in range(1, ways):
+        there = team * ways + lax.rem(spot + step, ways)
         copy = pltpu.make_async_remote_copy(
-            src_ref=k_mine, dst_ref=k_all.at[ka],
-            send_sem=k_ss.at[step], recv_sem=k_rs.at[ka],
+            src_ref=k_mine, dst_ref=k_all.at[spot],
+            send_sem=k_ss.at[step], recv_sem=k_rs.at[spot],
             device_id=(ph, there), device_id_type=MESH,
         )
         copy.start()
         k_copies.append(copy)
-    k_all[ka] = k_mine[...]
+    k_all[spot] = k_mine[...]
 
     def owned(owner, index):
         g, h = chunks[index]
@@ -155,8 +175,8 @@
                 g_copies[cell, tile + 1].wait()
                 right = jnp.concatenate(
                     [
-                        g_buf[cell, tile].reshape(depth, LANES),
-                        g_buf[cell, tile + 1].reshape(depth, LANES),
+                        g_buf.at[cell, tile].reshape(depth, LANES)[...],
+                        g_buf.at[cell, tile + 1].reshape(depth, LANES)[...],
                     ],
                     1,
                 )
@@ -209,19 +229,21 @@
                 ]
         for group in range(msplit):
             for local in range(here):
-                there = group * wsplit + h * here + lax.rem(local + ka, here)
-
-                @pl.when(there != ka)
-                def _():
-                    pltpu.make_async_remote_copy(
-                        src_ref=vert_send.at[there, g], dst_ref=vert_recv.at[ka, g],
-                        send_sem=v_ss.at[there, g], recv_sem=v_rs.at[ka, g],
-                        device_id=(ph, there), device_id_type=MESH,
-                    ).start()
-
-                @pl.when(there == ka)
-                def _():
-                    vert_recv[ka, g] = vert_send[there, g]
+                block = group * wsplit + h * here + lax.rem(local + spot, here)
+                for step in range(nka // ways - 1, -1, -1):
+                    there = lax.rem(team + step, nka // ways) * ways + block
+
+                    @pl.when(there != ka)
+                    def _():
+                        pltpu.make_async_remote_copy(
+                            src_ref=vert_send.at[block, g], dst_ref=vert_recv.at[ka, g],
+                            send_sem=v_ss.at[there, g], recv_sem=v_rs.at[ka, g],
+                            device_id=(ph, there), device_id_type=MESH,
+                        ).start()
+
+                    @pl.when(there == ka)
+                    def _():
+                        vert_recv[ka, g] = vert_send[block, g]
 
     count = len(chunks)
     for index in range(count):
@@ -235,54 +257,57 @@
     for index in range(max(count - 3, 0), count - 1):
         vertices(index)
 
-    for step in range(1, nka):
-        src = lax.rem(ka + step, nka)
+    for step in range(1, ways):
+        src = lax.rem(spot + step, ways)
         pltpu.make_async_remote_copy(
             src_ref=k_mine, dst_ref=k_all.at[src],
             send_sem=k_ss.at[step], recv_sem=k_rs.at[src],
-            device_id=(ph, src), device_id_type=MESH,
+            device_id=(ph, team * ways + src), device_id_type=MESH,
         ).wait_recv()
     el_cells = jnp.concatenate(
         [cell_ref[...].astype(jnp.float32), jnp.zeros((5, all_cells), jnp.float32)], 0
     )
 
     def phases(src, carry):
-        angle = turn(
+        cosine, sine = cos_sin(
             lax.dot_general(
                 el_cells, k_all[src], (((0,), (0,)), ((), ())), preferred_element_type=jnp.float32
             )
         )
-        cosine, sine = jnp.cos(angle), jnp.sin(angle)
         cos_re[src] = jnp.concatenate([cosine, -sine], 0).astype(jnp.bfloat16)
         cos_im[src] = jnp.concatenate([sine, cosine], 0).astype(jnp.bfloat16)
         return carry
 
-    lax.fori_loop(0, nka, phases, 0)
+    lax.fori_loop(0, ways, phases, 0)
     vertices(count - 1)
 
     for step in range(1, nka):
         src = lax.rem(ka + step, nka)
         for g in range(groups):
             pltpu.make_async_remote_copy(
-                src_ref=vert_send.at[src, g], dst_ref=vert_recv.at[src, g],
+                src_ref=vert_send.at[lax.rem(src, ways), g], dst_ref=vert_recv.at[src, g],
                 send_sem=v_ss.at[src, g], recv_sem=v_rs.at[src, g],
                 device_id=(ph, src), device_id_type=MESH,
             ).wait()
     for src in range(nka):
         for g in range(groups):
             at = src * block_rows + g * group_rows
-            vert_f32[at : at + group_rows, :] = vert_recv[src, g].astype(jnp.float32)
+            block = vert_recv[src, g].astype(jnp.float32)
+            for tile in range(vert_f32.shape[0]):
+                vert_f32[tile, at : at + group_rows, :] = block[:, tile * lanes : (tile + 1) * lanes]
     for mode in range(modes):
-        re_rows = vert_f32[pl.ds(mode, all_cells, stride=grouped), :]
-        im_rows = vert_f32[pl.ds(modes + mode, all_cells, stride=grouped), :]
-        turned[mode * wblk : (mode + 1) * wblk, :] = (
-            jnp.concatenate([re_rows, im_rows], 0).T.astype(jnp.bfloat16)
-        )
-
-    batch = 4 if modes % 4 == 0 else 1
+        for tile in range(vert_f32.shape[0]):
+            re_rows = vert_f32[tile, pl.ds(mode, all_cells, stride=grouped), :]
+            im_rows = vert_f32[tile, pl.ds(modes + mode, all_cells, stride=grouped), :]
+            at = mode * wblk + tile * lanes
+            turned[at : at + lanes, :] = (
+                jnp.concatenate([re_rows, im_rows], 0).T.astype(jnp.bfloat16)
+            )
+
+    batch = 2 if modes % 2 == 0 else 1
 
     def strengths(step, carry):
-        there = lax.rem(ka + step + 1, nka)
+        there = lax.rem(spot + step + 1, ways)
         phase_re, phase_im = cos_re[there], cos_im[there]
         for mode in range(0, modes, batch):
             left = turned[mode * wblk : (mode + batch) * wblk, :]
@@ -293,17 +318,17 @@
                 jnp.sum(squares.reshape(batch * nloc, W, kdev), axis=1) / normalizer
             )
 
-        @pl.when(step < nka - 1)
+        @pl.when(step < ways - 1)
         def _():
             pltpu.make_async_remote_copy(
-                src_ref=str_send.at[there], dst_ref=str_recv.at[ka],
-                send_sem=s_ss.at[there], recv_sem=s_rs.at[ka],
-                device_id=(ph, there), device_id_type=MESH,
+                src_ref=str_send.at[there], dst_ref=str_recv.at[spot],
+                send_sem=s_ss.at[there], recv_sem=s_rs.at[spot],
+                device_id=(ph, team * ways + there), device_id_type=MESH,
             ).start()
 
         return carry
 
-    lax.fori_loop(0, nka, strengths, 0)
+    lax.fori_loop(0, ways, strengths, 0)
 
     def place(src, held):
         group, piece = divmod(src, wsplit)
@@ -312,15 +337,15 @@
                 src, mode * nloc : (mode + 1) * nloc, :
             ]
 
-    str_recv[ka] = str_send[ka]
-    for step in range(1, nka):
-        src = lax.rem(ka + step, nka)
+    str_recv[spot] = str_send[spot]
+    for step in range(1, ways):
+        src = lax.rem(spot + step, ways)
         pltpu.make_async_remote_copy(
             src_ref=str_send.at[src], dst_ref=str_recv.at[src],
             send_sem=s_ss.at[src], recv_sem=s_rs.at[src],
-            device_id=(ph, src), device_id_type=MESH,
+            device_id=(ph, team * ways + src), device_id_type=MESH,
         ).wait()
-    for src in range(nka):
+    for src in range(ways):
         place(src, str_recv)
     for copy in list(core_copies.values()) + list(x_copies.values()) + k_copies:
         copy.wait_send()
@@ -331,12 +356,14 @@
     cells, ph_loc, disp, parts, width = g_wan.shape
     tiles = width // LANES
     g_view = g_wan.reshape(cells, ph_loc * disp, parts, tiles, LANES).transpose(0, 1, 3, 2, 4)
-    wsplit, msplit = splits(nka, width)
+    ways = team_size(nka)
+    wsplit, msplit = splits(ways, width)
     mode_total = eigvec.shape[-1]
     modes = mode_total // nph
     kdev, all_cells = kpoints.shape[1], el_cells.shape[1]
     nx, wblk = nph // 2, width // wsplit
     nloc = wblk // W
+    lanes = math.gcd(wblk, LANES)
     mode_group = modes // msplit
     block_rows = cells * 2 * mode_group
     groups = cell_groups(cells, 2 * mode_group)
@@ -363,23 +390,23 @@
             vmem(sent, bf16),
             vmem(passed, bf16),
             vmem(passed, bf16),
+            vmem((ways, groups, group_rows, wblk), bf16),
             vmem((nka, groups, group_rows, wblk), bf16),
-            vmem((nka, groups, group_rows, wblk), bf16),
-            vmem((nka * block_rows, wblk), f32),
+            vmem((wblk // lanes, nka * block_rows, lanes), f32),
             vmem((mode_group * wblk, 2 * all_cells), bf16),
             vmem((8, kdev), f32),
-            vmem((nka, 8, kdev), f32),
-            vmem((nka, 2 * all_cells, kdev), bf16),
-            vmem((nka, 2 * all_cells, kdev), bf16),
-            vmem((nka, mode_group * nloc, kdev), f32),
-            vmem((nka, mode_group * nloc, kdev), f32),
+            vmem((ways, 8, kdev), f32),
+            vmem((ways, 2 * all_cells, kdev), bf16),
+            vmem((ways, 2 * all_cells, kdev), bf16),
+            vmem((ways, mode_group * nloc, kdev), f32),
+            vmem((ways, mode_group * nloc, kdev), f32),
             dma((cells, tiles)),
             dma(sent[:2]), dma(sent[:2]), dma(passed[:2]), dma(passed[:2]),
             dma((nka, groups)), dma((nka, groups)),
-            dma((nka,)), dma((nka,)), dma((nka,)), dma((nka,)),
+            dma((ways,)), dma((ways,)), dma((ways,)), dma((ways,)),
         ],
         compiler_params=pltpu.CompilerParams(
-            collective_id=0, has_side_effects=True, vmem_limit_bytes=56 * 1024 * 1024
+            collective_id=0, has_side_effects=True, vmem_limit_bytes=52 * 1024 * 1024
         ),
     )(g_view, kpoints, el_cells, q_point, ph_cells, eigvec, omega.reshape(1, mode_total))
 

time: 36.1 us -> 36.6 us (1.014)
  local copies, waits for them, and re-layouts: 1.77 us -> 4.9 us
  Pallas kernels: 34.1 us -> 31.4 us
    unnamed x1 -> x13, local copies, waits for them, and re-layouts: 1.77 us -> 4.9 us
    pallas_call x1, Pallas kernels: 34.1 us -> 31.4 us  [shards(): pl.pallas_call(functools.partial(kernel, nph, nka, normalizer), out_shape...]
where the time goes in v3:
time: 36.6 us; the launch traced here: 36.3 us
  Pallas kernels  31.4 us (86%)
  local copies, waits for them, and re-layouts  4.9 us (13%)
    pallas_call x1, Pallas kernels, shards(): pl.pallas_call(functools.partial(kernel, nph, nka, normalizer), out_shape...  31.4 us
    unnamed x13, local copies, waits for them, and re-layouts  4.9 us

profile of v3, /device:TPU:0, one launch (start us, length us, event | category | flops | bytes accessed | tf_op | source)
XLA Modules:
  0.0 36.3 jit_solution(6334771046312866787)
XLA Ops:
  0.0 0.0 copy-start
  0.0 0.8 %copy-done = f32[2,48,48]{2,1,0:T(8,128)S(1)} copy-done((f32[2,48,48]{2,1,0:T(8,128)S(1)}, f32[2,48,48]{2,1,0:T(8,128)}, u32[]{:S(2)}) %copy-start) | copy-done | bytes 18456
  0.8 0.0 copy-start.1
  0.8 0.7 %copy-done.1 = s32[3,256]{1,0:T(4,128)S(1)} copy-done((s32[3,256]{1,0:T(4,128)S(1)}, s32[3,256]{1,0:T(4,128)}, u32[]{:S(2)}) %copy-start.1) | copy-done | bytes 3096
  1.5 0.0 copy-start.2
  1.5 0.7 %copy-done.2 = s32[3,32]{1,0:T(4,128)S(1)} copy-done((s32[3,32]{1,0:T(4,128)S(1)}, s32[3,32]{1,0:T(4,128)}, u32[]{:S(2)}) %copy-start.2) | copy-done | bytes 408
  2.2 0.0 copy-start.3
  2.2 0.7 %copy-done.3 = s32[3,12]{1,0:T(4,128)S(1)} copy-done((s32[3,12]{1,0:T(4,128)S(1)}, s32[3,12]{1,0:T(4,128)}, u32[]{:S(2)}) %copy-start.3) | copy-done | bytes 168
  2.9 0.0 copy-start.4
  2.9 0.7 %copy-done.4 = s32[3]{0:T(128)S(1)} copy-done((s32[3]{0:T(128)S(1)}, s32[3]{0:T(128)}, u32[]{:S(2)}) %copy-start.4) | copy-done | bytes 36
  3.5 0.0 copy-start.5
  3.5 0.7 %copy-done.5 = f32[48]{0:T(128)S(1)} copy-done((f32[48]{0:T(128)S(1)}, f32[48]{0:T(128)}, u32[]{:S(2)}) %copy-start.5) | copy-done | bytes 216
  4.2 31.4 %shard_map.73 = f32[12,32,256]{2,1,0:T(8,128)S(1)} custom-call(bf16[4,576,8,2,128]{4,3,2,1,0:T(2,128)(2,1)} %bitcast.5, s32[3,256]{1,0:T(4,128)S(1)} %copy-done.1, s32[3,32]{1,0:T(4,128)S(1)} %copy-done.2, s32[3]{0:T(128)S(1)} %copy-done.4, s32[3,12]{1,0:T(4,128)S(1)} %copy-done.3, f32[2,48,48]{2,1,0:T(8,128)S(1)} %copy-done, f32[1,48]{1,0:T(1,128)S(1)} %bitcast.4), custom_call_target="tpu_custom_call" | custom-call | tf_op jit(solution)/shard_map/pallas_call | solution.py:378
  35.6 0.7 %copy.9 = f32[12,32,256]{2,1,0:T(8,128)} copy(f32[12,32,256]{2,1,0:T(8,128)S(1)} %shard_map.73) | data formatting | bytes 786432
Async XLA Ops:
  0.0 0.8 %copy-start = (f32[2,48,48]{2,1,0:T(8,128)S(1)}, f32[2,48,48]{2,1,0:T(8,128)}, u32[]{:S(2)}) copy-start(f32[2,48,48]{2,1,0:T(8,128)} %eig_ref.1) | copy-start | bytes 55300
  0.8 0.7 %copy-start.1 = (s32[3,256]{1,0:T(4,128)S(1)}, s32[3,256]{1,0:T(4,128)}, u32[]{:S(2)}) copy-start(s32[3,256]{1,0:T(4,128)} %kpt_ref.1) | copy-start | bytes 9220
  1.5 0.7 %copy-start.2 = (s32[3,32]{1,0:T(4,128)S(1)}, s32[3,32]{1,0:T(4,128)}, u32[]{:S(2)}) copy-start(s32[3,32]{1,0:T(4,128)} %cell_ref.1) | copy-start | bytes 1156
  2.2 0.7 %copy-start.3 = (s32[3,12]{1,0:T(4,128)S(1)}, s32[3,12]{1,0:T(4,128)}, u32[]{:S(2)}) copy-start(s32[3,12]{1,0:T(4,128)} %phc_ref.1) | copy-start | bytes 436
  2.9 0.7 %copy-start.4 = (s32[3]{0:T(128)S(1)}, s32[3]{0:T(128)}, u32[]{:S(2)}) copy-start(s32[3]{0:T(128)} %q_ref.1) | copy-start | bytes 40
  3.5 0.7 %copy-start.5 = (f32[48]{0:T(128)S(1)}, f32[48]{0:T(128)}, u32[]{:S(2)}) copy-start(f32[48]{0:T(128)} %param.13) | copy-start | bytes 580

commit v4 on v3

--- a/solution.py
+++ b/solution.py
@@ -25,6 +25,10 @@
 
 def cell_groups(cells, grouped):
     return 2 if cells % 2 == 0 and (cells // 2 * grouped) % 16 == 0 else 1
+
+
+def lands_in_place(nloc, msplit):
+    return nloc % 8 == 0 and msplit == 1
 
 
 def cos_sin(numerator):
@@ -47,7 +51,8 @@
 
 
 def kernel(
-    nph, nka, normalizer, g_ref, kpt_ref, cell_ref, q_ref, phc_ref, eig_ref, omega_ref, out_ref,
+    nph, nka, normalizer, g_ref, kpt_hbm, cell_hbm, q_hbm, phc_hbm, eig_hbm, omega_hbm, out_ref,
+    kpt_ref, cell_ref, q_ref, phc_ref, eig_ref, omega_ref, small_sem,
     g_buf, table, part, core_send, core_recv, x_send, x_recv, vert_send, vert_recv, vert_f32, turned,
     k_mine, k_all, cos_re, cos_im, str_send, str_recv,
     g_sem, core_ss, core_rs, x_ss, x_rs, v_ss, v_rs, k_ss, k_rs, s_ss, s_rs,
@@ -68,6 +73,7 @@
     modes = grouped // 2
     wblk = width // wsplit
     nloc = wblk // W
+    direct = lands_in_place(nloc, msplit)
     lanes = vert_f32.shape[2]
     block_rows = cells * grouped
     groups = cell_groups(cells, grouped)
@@ -83,7 +89,9 @@
     chunks = [(g, h) for g in range(groups) for h in range(halves)]
     tiles_half = tiles // halves
     g_copies = {}
-    for g, h in chunks:
+
+    def fetch(index):
+        g, h = chunks[index]
         for cell in range(g * group_cells, (g + 1) * group_cells):
             for tile in range(h * tiles_half, (h + 1) * tiles_half):
                 copy = pltpu.make_async_copy(
@@ -91,6 +99,19 @@
                 )
                 copy.start()
                 g_copies[cell, tile] = copy
+
+    small = []
+    for at, (src, dst) in enumerate(
+        [
+            (eig_hbm, eig_ref), (omega_hbm, omega_ref), (q_hbm, q_ref),
+            (phc_hbm, phc_ref), (kpt_hbm, kpt_ref), (cell_hbm, cell_ref),
+        ]
+    ):
+        small.append(pltpu.make_async_copy(src, dst, small_sem.at[at]))
+        small[-1].start()
+    fetch(0)
+    if len(chunks) > 1:
+        fetch(1)
 
     barrier = pltpu.get_barrier_semaphore()
     pl.semaphore_signal(barrier, inc=1, device_id=(mate, ka), device_id_type=MESH)
@@ -101,6 +122,8 @@
         there = lax.rem(ka + step, nka)
         pl.semaphore_signal(barrier, inc=1, device_id=(ph, there), device_id_type=MESH)
 
+    for copy in small:
+        copy.wait()
     spread_v = lax.broadcasted_iota(jnp.int32, (disp, 2 * disp), 0)
     spread_col = lax.broadcasted_iota(jnp.int32, (disp, 2 * disp), 1)
     even = (spread_col == 2 * spread_v).astype(jnp.float32)
@@ -248,6 +271,8 @@
     count = len(chunks)
     for index in range(count):
         multiply(index)
+        if index + 2 < count:
+            fetch(index + 2)
         to_mate(index)
         if index >= 1:
             to_other_chips(index - 1)
@@ -314,19 +339,29 @@
             bloch_re = jnp.dot(left, phase_re, preferred_element_type=jnp.float32)
             bloch_im = jnp.dot(left, phase_im, preferred_element_type=jnp.float32)
             squares = bloch_re * bloch_re + bloch_im * bloch_im
-            str_send[there, mode * nloc : (mode + batch) * nloc, :] = (
-                jnp.sum(squares.reshape(batch * nloc, W, kdev), axis=1) / normalizer
-            )
+            summed = jnp.sum(squares.reshape(batch * nloc, W, kdev), axis=1) * (1.0 / normalizer)
+            if direct:
+                str_send[there, mode : mode + batch] = summed.reshape(batch, nloc, kdev)
+            else:
+                str_send[there, mode * nloc : (mode + batch) * nloc, :] = summed
 
         @pl.when(step < ways - 1)
         def _():
-            pltpu.make_async_remote_copy(
-                src_ref=str_send.at[there], dst_ref=str_recv.at[spot],
-                send_sem=s_ss.at[there], recv_sem=s_rs.at[spot],
-                device_id=(ph, team * ways + there), device_id_type=MESH,
-            ).start()
+            strength_copy(there, there, spot).start()
 
         return carry
+
+    def landing(src):
+        if direct:
+            return out_ref.at[:, pl.ds(pl.multiple_of(src * nloc, 8), nloc), :]
+        return str_recv.at[src]
+
+    def strength_copy(there, sem, src):
+        return pltpu.make_async_remote_copy(
+            src_ref=str_send.at[there], dst_ref=landing(src),
+            send_sem=s_ss.at[sem], recv_sem=s_rs.at[src],
+            device_id=(ph, team * ways + there), device_id_type=MESH,
+        )
 
     lax.fori_loop(0, ways, strengths, 0)
 
@@ -337,16 +372,19 @@
                 src, mode * nloc : (mode + 1) * nloc, :
             ]
 
-    str_recv[spot] = str_send[spot]
+    if direct:
+        own = pltpu.make_async_copy(str_send.at[spot], landing(spot), s_rs.at[spot])
+        own.start()
+    else:
+        str_recv[spot] = str_send[spot]
     for step in range(1, ways):
         src = lax.rem(spot + step, ways)
-        pltpu.make_async_remote_copy(
-            src_ref=str_send.at[src], dst_ref=str_recv.at[src],
-            send_sem=s_ss.at[src], recv_sem=s_rs.at[src],
-            device_id=(ph, team * ways + src), device_id_type=MESH,
-        ).wait()
-    for src in range(ways):
-        place(src, str_recv)
+        strength_copy(src, src, src).wait()
+    if direct:
+        own.wait()
+    else:
+        for src in range(ways):
+            place(src, str_recv)
     for copy in list(core_copies.values()) + list(x_copies.values()) + k_copies:
         copy.wait_send()
 
@@ -364,6 +402,8 @@
     nx, wblk = nph // 2, width // wsplit
     nloc = wblk // W
     lanes = math.gcd(wblk, LANES)
+    direct = lands_in_place(nloc, msplit)
+    strength_block = (modes, nloc, kdev) if direct else (modes // msplit * nloc, kdev)
     mode_group = modes // msplit
     block_rows = cells * 2 * mode_group
     groups = cell_groups(cells, 2 * mode_group)
@@ -373,16 +413,20 @@
     passed = (chunks, nx - 1, msplit * group_rows, width // 2)
     bf16, f32 = jnp.bfloat16, jnp.float32
     vmem, dma = pltpu.VMEM, pltpu.SemaphoreType.DMA
-    in_vmem, in_smem = pl.BlockSpec(memory_space=vmem), pl.BlockSpec(memory_space=pltpu.SMEM)
     normalizer = float(all_cells * ph_loc * nph * W)
     return pl.pallas_call(
         functools.partial(kernel, nph, nka, normalizer),
         out_shape=jax.ShapeDtypeStruct((modes, W, kdev), f32),
-        in_specs=[
-            pl.BlockSpec(memory_space=pl.ANY), in_vmem, in_vmem, in_smem, in_vmem, in_vmem, in_vmem
-        ],
-        out_specs=in_vmem,
+        in_specs=[pl.BlockSpec(memory_space=pltpu.HBM)] * 7,
+        out_specs=pl.BlockSpec(memory_space=pltpu.HBM if direct else vmem),
         scratch_shapes=[
+            vmem(kpoints.shape, jnp.int32),
+            vmem(el_cells.shape, jnp.int32),
+            pltpu.SMEM(q_point.shape, jnp.int32),
+            vmem(ph_cells.shape, jnp.int32),
+            vmem(eigvec.shape, f32),
+            vmem((1, mode_total), f32),
+            dma((6,)),
             vmem((cells, tiles, ph_loc * disp, parts, LANES), bf16),
             vmem((2 * mode_total, ph_loc * disp * parts), bf16),
             vmem((cells, 2 * mode_total, width), f32),
@@ -398,15 +442,15 @@
             vmem((ways, 8, kdev), f32),
             vmem((ways, 2 * all_cells, kdev), bf16),
             vmem((ways, 2 * all_cells, kdev), bf16),
-            vmem((ways, mode_group * nloc, kdev), f32),
-            vmem((ways, mode_group * nloc, kdev), f32),
+            vmem((ways, *strength_block), f32),
+            vmem((8, LANES) if direct else (ways, *strength_block), f32),
             dma((cells, tiles)),
             dma(sent[:2]), dma(sent[:2]), dma(passed[:2]), dma(passed[:2]),
             dma((nka, groups)), dma((nka, groups)),
             dma((ways,)), dma((ways,)), dma((ways,)), dma((ways,)),
         ],
         compiler_params=pltpu.CompilerParams(
-            collective_id=0, has_side_effects=True, vmem_limit_bytes=52 * 1024 * 1024
+            collective_id=0, has_side_effects=True, vmem_limit_bytes=56 * 1024 * 1024
         ),
     )(g_view, kpoints, el_cells, q_point, ph_cells, eigvec, omega.reshape(1, mode_total))
 

time: 36.6 us -> 33.2 us (0.907)
  local copies, waits for them, and re-layouts: 4.9 us -> 1.77 us
    unnamed x13 -> x1, local copies, waits for them, and re-layouts: 4.9 us -> 1.77 us
where the time goes in v4:
time: 33.2 us; the launch traced here: 33 us
  Pallas kernels  31.3 us (94%)
  local copies, waits for them, and re-layouts  1.77 us (5%)
    pallas_call x1, Pallas kernels, shards(): pl.pallas_call(functools.partial(kernel, nph, nka, normalizer), out_shape...  31.3 us
    unnamed x1, local copies, waits for them, and re-layouts  1.77 us

profile of v4, /device:TPU:0, one launch (start us, length us, event | category | flops | bytes accessed | tf_op | source)
XLA Modules:
  0.0 33.0 jit_solution(13775610182526129946)
XLA Ops:
  0.0 31.3 %shard_map.73 = f32[12,32,256]{2,1,0:T(8,128)} custom-call(bf16[4,576,8,2,128]{4,3,2,1,0:T(2,128)(2,1)} %bitcast.4, s32[3,256]{1,0:T(4,128)} %kpt_hbm.1, s32[3,32]{1,0:T(4,128)} %cell_hbm.1, s32[3]{0:T(128)} %q_hbm.1, s32[3,12]{1,0:T(4,128)} %phc_hbm.1, f32[2,48,48]{2,1,0:T(8,128)} %eig_hbm.1, f32[1,48]{1,0:T(1,128)} %bitcast.5), custom_call_target="tpu_custom_call" | custom-call | tf_op jit(solution)/shard_map/pallas_call | solution.py:417
  31.3 1.8 %copy.9 = f32[12,32,256]{2,1,0:T(8,128)} copy(f32[12,32,256]{2,1,0:T(8,128)} %shard_map.73) | data formatting | bytes 786432

commit v5 on v4

--- a/solution.py
+++ b/solution.py
@@ -15,7 +15,7 @@
 
 
 def team_size(nka):
-    return nka // 2 if nka % 2 == 0 else nka
+    return nka
 
 
 def splits(ways, width):
@@ -27,8 +27,8 @@
     return 2 if cells % 2 == 0 and (cells // 2 * grouped) % 16 == 0 else 1
 
 
-def lands_in_place(nloc, msplit):
-    return nloc % 8 == 0 and msplit == 1
+def padded(rows):
+    return -(-rows // 16) * 16
 
 
 def cos_sin(numerator):
@@ -54,8 +54,8 @@
     nph, nka, normalizer, g_ref, kpt_hbm, cell_hbm, q_hbm, phc_hbm, eig_hbm, omega_hbm, out_ref,
     kpt_ref, cell_ref, q_ref, phc_ref, eig_ref, omega_ref, small_sem,
     g_buf, table, part, core_send, core_recv, x_send, x_recv, vert_send, vert_recv, vert_f32, turned,
-    k_mine, k_all, cos_re, cos_im, str_send, str_recv,
-    g_sem, core_ss, core_rs, x_ss, x_rs, v_ss, v_rs, k_ss, k_rs, s_ss, s_rs,
+    k_mine, k_all, cos_re, cos_im, str_send, str_recv, str_f32, mean_send, mean_recv,
+    g_sem, core_ss, core_rs, x_ss, x_rs, v_ss, v_rs, k_ss, k_rs, s_ss, s_rs, m_ss, m_rs,
 ):
     ph, ka = lax.axis_index("ph"), lax.axis_index("ka")
     nx = nph // 2
@@ -73,7 +73,7 @@
     modes = grouped // 2
     wblk = width // wsplit
     nloc = wblk // W
-    direct = lands_in_place(nloc, msplit)
+    str_rows = str_f32.shape[0]
     lanes = vert_f32.shape[2]
     block_rows = cells * grouped
     groups = cell_groups(cells, grouped)
@@ -278,9 +278,11 @@
             to_other_chips(index - 1)
         if index >= 3:
             vertices(index - 3)
+    for index in range(max(count - 3, 0), count - 2):
+        vertices(index)
     to_other_chips(count - 1)
-    for index in range(max(count - 3, 0), count - 1):
-        vertices(index)
+    if count > 1:
+        vertices(count - 2)
 
     for step in range(1, ways):
         src = lax.rem(spot + step, ways)
@@ -329,7 +331,7 @@
                 jnp.concatenate([re_rows, im_rows], 0).T.astype(jnp.bfloat16)
             )
 
-    batch = 2 if modes % 2 == 0 else 1
+    batch = 4 if modes % 4 == 0 else 1
 
     def strengths(step, carry):
         there = lax.rem(spot + step + 1, ways)
@@ -340,51 +342,53 @@
             bloch_im = jnp.dot(left, phase_im, preferred_element_type=jnp.float32)
             squares = bloch_re * bloch_re + bloch_im * bloch_im
             summed = jnp.sum(squares.reshape(batch * nloc, W, kdev), axis=1) * (1.0 / normalizer)
-            if direct:
-                str_send[there, mode : mode + batch] = summed.reshape(batch, nloc, kdev)
-            else:
-                str_send[there, mode * nloc : (mode + batch) * nloc, :] = summed
+            str_f32[mode * nloc : (mode + batch) * nloc, :] = summed
+        held = str_f32[...]
+        mean = jnp.sum(held, axis=1, keepdims=True) * (1.0 / kdev)
+        str_send[there] = (held - mean).astype(jnp.bfloat16)
+        mean_send[there, :, 0:str_rows] = jnp.broadcast_to(mean, (str_rows, LANES)).T[0:1, :]
 
         @pl.when(step < ways - 1)
         def _():
-            strength_copy(there, there, spot).start()
+            for copy in strength_copies(there, spot):
+                copy.start()
 
         return carry
 
-    def landing(src):
-        if direct:
-            return out_ref.at[:, pl.ds(pl.multiple_of(src * nloc, 8), nloc), :]
-        return str_recv.at[src]
-
-    def strength_copy(there, sem, src):
-        return pltpu.make_async_remote_copy(
-            src_ref=str_send.at[there], dst_ref=landing(src),
-            send_sem=s_ss.at[sem], recv_sem=s_rs.at[src],
-            device_id=(ph, team * ways + there), device_id_type=MESH,
-        )
-
+    def strength_copies(there, src):
+        return [
+            pltpu.make_async_remote_copy(
+                src_ref=outgoing.at[there], dst_ref=incoming.at[src],
+                send_sem=sent.at[there], recv_sem=got.at[src],
+                device_id=(ph, team * ways + there), device_id_type=MESH,
+            )
+            for outgoing, incoming, sent, got in (
+                (mean_send, mean_recv, m_ss, m_rs), (str_send, str_recv, s_ss, s_rs)
+            )
+        ]
+
+    str_f32[...] = jnp.zeros_like(str_f32)
+    mean_send[...] = jnp.zeros_like(mean_send)
     lax.fori_loop(0, ways, strengths, 0)
 
-    def place(src, held):
+    def place(src):
+        row = mean_recv[src][:, 0:str_rows]
+        mean = jnp.broadcast_to(row, (LANES, str_rows)).T[:, 0:1]
+        held = str_recv[src].astype(jnp.float32) + mean
         group, piece = divmod(src, wsplit)
         for mode in range(modes):
             out_ref[group * modes + mode, piece * nloc : (piece + 1) * nloc, :] = held[
-                src, mode * nloc : (mode + 1) * nloc, :
+                mode * nloc : (mode + 1) * nloc, :
             ]
 
-    if direct:
-        own = pltpu.make_async_copy(str_send.at[spot], landing(spot), s_rs.at[spot])
-        own.start()
-    else:
-        str_recv[spot] = str_send[spot]
+    str_recv[spot] = str_send[spot]
+    mean_recv[spot] = mean_send[spot]
     for step in range(1, ways):
         src = lax.rem(spot + step, ways)
-        strength_copy(src, src, src).wait()
-    if direct:
-        own.wait()
-    else:
-        for src in range(ways):
-            place(src, str_recv)
+        for copy in strength_copies(src, src):
+            copy.wait()
+    for src in range(ways):
+        place(src)
     for copy in list(core_copies.values()) + list(x_copies.values()) + k_copies:
         copy.wait_send()
 
@@ -402,8 +406,8 @@
     nx, wblk = nph // 2, width // wsplit
     nloc = wblk // W
     lanes = math.gcd(wblk, LANES)
-    direct = lands_in_place(nloc, msplit)
-    strength_block = (modes, nloc, kdev) if direct else (modes // msplit * nloc, kdev)
+    str_rows = padded(modes // msplit * nloc)
+    mean_lanes = -(-str_rows // LANES) * LANES
     mode_group = modes // msplit
     block_rows = cells * 2 * mode_group
     groups = cell_groups(cells, 2 * mode_group)
@@ -418,7 +422,7 @@
         functools.partial(kernel, nph, nka, normalizer),
         out_shape=jax.ShapeDtypeStruct((modes, W, kdev), f32),
         in_specs=[pl.BlockSpec(memory_space=pltpu.HBM)] * 7,
-        out_specs=pl.BlockSpec(memory_space=pltpu.HBM if direct else vmem),
+        out_specs=pl.BlockSpec(memory_space=vmem),
         scratch_shapes=[
             vmem(kpoints.shape, jnp.int32),
             vmem(el_cells.shape, jnp.int32),
@@ -442,12 +446,15 @@
             vmem((ways, 8, kdev), f32),
             vmem((ways, 2 * all_cells, kdev), bf16),
             vmem((ways, 2 * all_cells, kdev), bf16),
-            vmem((ways, *strength_block), f32),
-            vmem((8, LANES) if direct else (ways, *strength_block), f32),
+            vmem((ways, str_rows, kdev), bf16),
+            vmem((ways, str_rows, kdev), bf16),
+            vmem((str_rows, kdev), f32),
+            vmem((ways, 1, mean_lanes), f32),
+            vmem((ways, 1, mean_lanes), f32),
             dma((cells, tiles)),
             dma(sent[:2]), dma(sent[:2]), dma(passed[:2]), dma(passed[:2]),
             dma((nka, groups)), dma((nka, groups)),
-            dma((ways,)), dma((ways,)), dma((ways,)), dma((ways,)),
+            dma((ways,)), dma((ways,)), dma((ways,)), dma((ways,)), dma((ways,)), dma((ways,)),
         ],
         compiler_params=pltpu.CompilerParams(
             collective_id=0, has_side_effects=True, vmem_limit_bytes=56 * 1024 * 1024

time: 33.2 us -> 32.8 us (0.988)
  Pallas kernels: 31.3 us -> 30.8 us
    pallas_call x1, Pallas kernels: 31.3 us -> 30.8 us  [shards(): pl.pallas_call(functools.partial(kernel, nph, nka, normalizer), out_shape...]
where the time goes in v5:
time: 32.8 us; the launch traced here: 32.6 us
  Pallas kernels  30.8 us (94%)
  local copies, waits for them, and re-layouts  1.77 us (5%)
    pallas_call x1, Pallas kernels, shards(): pl.pallas_call(functools.partial(kernel, nph, nka, normalizer), out_shape...  30.8 us
    unnamed x1, local copies, waits for them, and re-layouts  1.77 us

profile of v5, /device:TPU:0, one launch (start us, length us, event | category | flops | bytes accessed | tf_op | source)
XLA Modules:
  0.0 32.6 jit_solution(10958651758584237596)
XLA Ops:
  0.0 30.8 %shard_map.73 = f32[12,32,256]{2,1,0:T(8,128)} custom-call(bf16[4,576,8,2,128]{4,3,2,1,0:T(2,128)(2,1)} %bitcast.4, s32[3,256]{1,0:T(4,128)} %kpt_hbm.1, s32[3,32]{1,0:T(4,128)} %cell_hbm.1, s32[3]{0:T(128)} %q_hbm.1, s32[3,12]{1,0:T(4,128)} %phc_hbm.1, f32[2,48,48]{2,1,0:T(8,128)} %eig_hbm.1, f32[1,48]{1,0:T(1,128)} %bitcast.5), custom_call_target="tpu_custom_call" | custom-call | tf_op jit(solution)/shard_map/pallas_call | solution.py:421
  30.8 1.8 %copy.9 = f32[12,32,256]{2,1,0:T(8,128)} copy(f32[12,32,256]{2,1,0:T(8,128)} %shard_map.73) | data formatting | bytes 786432

commit v6 on v5

--- a/solution.py
+++ b/solution.py
@@ -308,16 +308,17 @@
     lax.fori_loop(0, ways, phases, 0)
     vertices(count - 1)
 
-    for step in range(1, nka):
-        src = lax.rem(ka + step, nka)
-        for g in range(groups):
-            pltpu.make_async_remote_copy(
-                src_ref=vert_send.at[lax.rem(src, ways), g], dst_ref=vert_recv.at[src, g],
-                send_sem=v_ss.at[src, g], recv_sem=v_rs.at[src, g],
-                device_id=(ph, src), device_id_type=MESH,
-            ).wait()
     for src in range(nka):
         for g in range(groups):
+
+            @pl.when(src != ka)
+            def _():
+                pltpu.make_async_remote_copy(
+                    src_ref=vert_send.at[src % ways, g], dst_ref=vert_recv.at[src, g],
+                    send_sem=v_ss.at[src, g], recv_sem=v_rs.at[src, g],
+                    device_id=(ph, src), device_id_type=MESH,
+                ).wait()
+
             at = src * block_rows + g * group_rows
             block = vert_recv[src, g].astype(jnp.float32)
             for tile in range(vert_f32.shape[0]):
@@ -334,7 +335,8 @@
     batch = 4 if modes % 4 == 0 else 1
 
     def strengths(step, carry):
-        there = lax.rem(spot + step + 1, ways)
+        reach = lax.div(step + 1, 2)
+        there = lax.rem(spot + ways // 2 + reach - 2 * reach * lax.rem(step, 2), ways)
         phase_re, phase_im = cos_re[there], cos_im[there]
         for mode in range(0, modes, batch):
             left = turned[mode * wblk : (mode + batch) * wblk, :]
@@ -348,7 +350,7 @@
         str_send[there] = (held - mean).astype(jnp.bfloat16)
         mean_send[there, :, 0:str_rows] = jnp.broadcast_to(mean, (str_rows, LANES)).T[0:1, :]
 
-        @pl.when(step < ways - 1)
+        @pl.when(there != spot)
         def _():
             for copy in strength_copies(there, spot):
                 copy.start()
@@ -383,11 +385,13 @@
 
     str_recv[spot] = str_send[spot]
     mean_recv[spot] = mean_send[spot]
-    for step in range(1, ways):
-        src = lax.rem(spot + step, ways)
-        for copy in strength_copies(src, src):
-            copy.wait()
     for src in range(ways):
+
+        @pl.when(src != spot)
+        def _():
+            for copy in strength_copies(src, src):
+                copy.wait()
+
         place(src)
     for copy in list(core_copies.values()) + list(x_copies.values()) + k_copies:
         copy.wait_send()

time: 32.8 us -> 35.3 us (1.076)
  Pallas kernels: 30.8 us -> 33.4 us
    pallas_call x1, Pallas kernels: 30.8 us -> 33.4 us  [shards(): pl.pallas_call(functools.partial(kernel, nph, nka, normalizer), out_shape...]
where the time goes in v6:
time: 35.3 us; the launch traced here: 35.2 us
  Pallas kernels  33.4 us (95%)
  local copies, waits for them, and re-layouts  1.77 us (5%)
    pallas_call x1, Pallas kernels, shards(): pl.pallas_call(functools.partial(kernel, nph, nka, normalizer), out_shape...  33.4 us
    unnamed x1, local copies, waits for them, and re-layouts  1.77 us

profile of v6, /device:TPU:0, one launch (start us, length us, event | category | flops | bytes accessed | tf_op | source)
XLA Modules:
  0.0 35.2 jit_solution(1782623747569438275)
XLA Ops:
  0.0 33.4 %shard_map.73 = f32[12,32,256]{2,1,0:T(8,128)} custom-call(bf16[4,576,8,2,128]{4,3,2,1,0:T(2,128)(2,1)} %bitcast.4, s32[3,256]{1,0:T(4,128)} %kpt_hbm.1, s32[3,32]{1,0:T(4,128)} %cell_hbm.1, s32[3]{0:T(128)} %q_hbm.1, s32[3,12]{1,0:T(4,128)} %phc_hbm.1, f32[2,48,48]{2,1,0:T(8,128)} %eig_hbm.1, f32[1,48]{1,0:T(1,128)} %bitcast.5), custom_call_target="tpu_custom_call" | custom-call | tf_op jit(solution)/shard_map/pallas_call | solution.py:425
  33.4 1.8 %copy.9 = f32[12,32,256]{2,1,0:T(8,128)} copy(f32[12,32,256]{2,1,0:T(8,128)} %shard_map.73) | data formatting | bytes 786432
